TPU v7x, 256 devices: a whole 4x4x8 slice. The times are simulated.
256 devices in a mesh: ep: 8 (over y, core), seq: 32 (over z, x).
Axes of the slice: x: 4, y: 4, z: 8, core: 2. Of those that a mesh axis runs over, the one named last changes fastest.
Arguments:
- frames: bfloat16 [8, 22528, 512], P('ep', 'seq'), may hold values from -6 to 6
- lengths: int32 [8], P('ep'), may hold values from 11264 to 22528
- w_in: bfloat16 [512, 1024], replicated, may hold values from -0.25 to 0.25
- kernel: float32 [31, 512], replicated, may hold values from -1 to 1
- w_out: bfloat16 [512, 512], replicated, may hold values from -0.25 to 0.25
- pool_query: bfloat16 [8, 512], replicated, may hold values from -600 to 600
- w_value: bfloat16 [512, 512], replicated, may hold values from -0.25 to 0.25
- text_emb: bfloat16 [256, 512], replicated, may hold values from -6 to 6
- teacher: float32 [8, 256], P('ep'), may hold values from -6 to 6
Outputs:
- loss: float32 [], replicated
- grad_in: float32 [512, 1024], P('seq', 'ep')
- grad_out: float32 [512, 512], P('seq', 'ep')
- grad_kernel: float32 [31, 512], replicated
- grad_query: float32 [8, 512], replicated
- grad_value: float32 [512, 512], replicated
All inputs are finite; a program needn't handle non-finite values.
Results may differ from a plain program's by a relative error of at most 0.03.
Values may be sent and summed in bfloat16 or wider, within the bound.
No kernel may reach another device: no remote copies, remote signals or barrier semaphores. Data moves between devices by JAX's collectives and lax.ppermute only.
A program may use at most 64 MiB of HBM per device.

v0:
```python
import jax
import jax.numpy as jnp
from jax import lax
from jax.sharding import PartitionSpec as P


def padded_2(block, sides, width):
    for axis, dim in sides:
        count = lax.axis_size(axis)
        forward = [(i, i + 1) for i in range(count - 1)]
        backward = [(target, source) for source, target in forward]
        low = lax.ppermute(
            lax.slice_in_dim(block, block.shape[dim] - width, None, axis=dim), axis, forward
        )
        high = lax.ppermute(lax.slice_in_dim(block, 0, width, axis=dim), axis, backward)
        block = jnp.concatenate([low, block, high], axis=dim)
    return block


def shards(frames, lengths, w_in, kernel, w_out, pool_query, w_value, text_emb, teacher):
    hi = lax.Precision.HIGHEST
    n_epis, n_rows, width = frames.shape
    n_taps = kernel.shape[0]
    rim = n_taps // 2
    n_heads = pool_query.shape[0]
    head_dim = width // n_heads
    n_cands = text_emb.shape[0]
    root_width = jnp.sqrt(jnp.float32(width))
    offset = lax.axis_index("seq") * n_rows
    positions = offset + jnp.arange(n_rows, dtype=jnp.int32)
    valid = (positions[None, :] < lengths[:, None]).astype(jnp.float32)[..., None]
    xf = frames.astype(jnp.float32)
    mean_val = jnp.mean(xf, axis=-1, keepdims=True)
    var_val = jnp.mean((xf - mean_val) ** 2, axis=-1, keepdims=True)
    normed = ((xf - mean_val) * lax.rsqrt(var_val + 1e-05)).astype(jnp.bfloat16)
    mixed = jnp.einsum("esd,df->esf", normed, w_in, preferred_element_type=jnp.float32)
    sig = jax.nn.sigmoid(mixed[..., width:])
    glu = (mixed[..., :width] * sig * valid).astype(jnp.bfloat16)
    padded = padded_2(glu, (("seq", 1),), rim)
    conv = jnp.zeros((n_epis, n_rows, width), jnp.float32)
    for k in range(n_taps):
        conv = conv + kernel[k] * padded[:, k : k + n_rows].astype(jnp.float32)
    sconv = jax.nn.sigmoid(conv)
    act = (conv * sconv).astype(jnp.bfloat16)
    resid = xf + jnp.einsum("esd,df->esf", act, w_out, preferred_element_type=jnp.float32)
    queries = pool_query.astype(jnp.float32)
    scores = jnp.einsum("esd,hd->esh", resid, queries, precision=hi) / root_width
    masked = jnp.where(valid > 0, scores, -1e30)
    top = lax.pmax(jnp.max(masked, axis=1), "seq")
    expo = jnp.where(valid > 0, jnp.exp(masked - top[:, None]), 0.0)
    vec_here = jnp.einsum("esh,esd->ehd", expo, resid, precision=hi)
    total, vec = lax.psum((jnp.sum(expo, axis=1), vec_here), "seq")
    probs = jnp.where(valid > 0, jnp.exp(masked - top[:, None]), 0.0) / total[:, None]
    vbar = vec / total[..., None]
    wvals = w_value.astype(jnp.float32).reshape(width, n_heads, head_dim)
    pooled = jnp.einsum("ehd,dhk->ehk", vbar, wvals, precision=hi).reshape(n_epis, width)
    rms = jnp.sqrt(jnp.mean(pooled * pooled, axis=-1, keepdims=True) + 1e-06)
    emb = pooled / rms
    texts = text_emb.astype(jnp.float32)
    score = jnp.einsum("ed,cd->ec", emb, texts, precision=hi) / root_width
    diff = score - teacher
    loss_here = jnp.sum(diff * diff) / n_cands
    dscore = 2.0 * diff / n_cands
    demb = jnp.einsum("ec,cd->ed", dscore, texts, precision=hi) / root_width
    dpooled = (demb - emb * jnp.mean(demb * emb, axis=-1, keepdims=True)) / rms
    dp3 = dpooled.reshape(n_epis, n_heads, head_dim)
    value_here = jnp.einsum("ehd,ehk->dhk", vbar, dp3, precision=hi).reshape(width, width)
    dvbar = jnp.einsum("dhk,ehk->ehd", wvals, dp3, precision=hi)
    proj = jnp.einsum("esd,ehd->esh", resid, dvbar, precision=hi)
    centre = jnp.sum(dvbar * vbar, axis=-1)
    dscores = probs * (proj - centre[:, None])
    query_here = jnp.einsum("esh,esd->hd", dscores, resid, precision=hi) / root_width
    dresid = (
        jnp.einsum("esh,ehd->esd", probs, dvbar, precision=hi)
        + jnp.einsum("esh,hd->esd", dscores, queries, precision=hi) / root_width
    ).astype(jnp.bfloat16)
    out_here = jnp.einsum("esd,esf->df", act, dresid, preferred_element_type=jnp.float32)
    dact = jnp.einsum("esf,df->esd", dresid, w_out, preferred_element_type=jnp.float32)
    dconv = (dact * sconv * (1.0 + conv * (1.0 - sconv))).astype(jnp.bfloat16)
    dconv_f = dconv.astype(jnp.float32)
    dpad = padded_2(dconv, (("seq", 1),), rim)
    dglu = jnp.zeros((n_epis, n_rows, width), jnp.float32)
    taps = []
    for k in range(n_taps):
        dglu = dglu + kernel[k] * dpad[:, 2 * rim - k : 2 * rim - k + n_rows].astype(jnp.float32)
        taps.append(jnp.sum(padded[:, k : k + n_rows].astype(jnp.float32) * dconv_f, axis=(0, 1)))
    kernel_here = jnp.stack(taps)
    dglu = dglu * valid
    dmixed = jnp.concatenate(
        [dglu * sig, dglu * mixed[..., :width] * sig * (1.0 - sig)], axis=-1
    ).astype(jnp.bfloat16)
    in_here = jnp.einsum("esd,esf->df", normed, dmixed, preferred_element_type=jnp.float32)
    rows_in, rows_out = (
        lax.psum_scatter(
            in_here.astype(jnp.bfloat16), "seq", scatter_dimension=0, tiled=True
        ).astype(jnp.float32),
        lax.psum_scatter(
            out_here.astype(jnp.bfloat16), "seq", scatter_dimension=0, tiled=True
        ).astype(jnp.float32),
    )
    grad_in, grad_out = (
        lax.psum_scatter(
            rows_in.astype(jnp.bfloat16), "ep", scatter_dimension=1, tiled=True
        ).astype(jnp.float32),
        lax.psum_scatter(
            rows_out.astype(jnp.bfloat16), "ep", scatter_dimension=1, tiled=True
        ).astype(jnp.float32),
    )
    grad_kernel, grad_query = lax.psum((kernel_here, query_here), ("ep", "seq"))
    grad_value, loss = (
        lax.psum(value_here.astype(jnp.bfloat16), "ep").astype(jnp.float32),
        lax.psum(loss_here.astype(jnp.bfloat16), "ep").astype(jnp.float32),
    )
    return (loss, grad_in, grad_out, grad_kernel, grad_query, grad_value)


def solution(mesh):
    return jax.shard_map(
        shards,
        mesh=mesh,
        in_specs=(P("ep", "seq", None), P("ep"), P(), P(), P(), P(), P(), P(), P("ep", None)),
        out_specs=(P(), P("seq", "ep"), P("seq", "ep"), P(), P(), P()),
        check_vma=False,
    )
```

profile of v0, /device:TPU:1, one launch (start us, length us, event | category | flops | bytes accessed | tf_op | source)
XLA Modules:
  0.0 1106.2 jit_solution(10548095060268716896)
XLA Ops:
  9.3 1.5 fusion.5
  14.0 3.9 collective-permute-start
  20.6 1.8 collective-permute-done.1
  22.6 9.4 fusion.36
  34.1 62.9 %pmax.7 = f32[8]{0:T(128)S(1)} all-reduce(f32[8]{0:T(128)S(1)} %get-tuple-element.101), channel_id=1, replica_groups=mesh['ep'=8,'seq'=32] {'seq'}, use_global_device_ids=true, to_apply=%region_3.4 | all-reduce | flops 8 | bytes 64 | tf_op jit(solution)/shard_map/pmax | solution.py:49
  98.5 111.0 %all-reduce.1 = (f32[1,8,512]{2,1,0:T(8,128)}, f32[8]{0:T(128)S(1)}) all-reduce(f32[1,8,512]{2,1,0:T(8,128)S(1)} %convolution_bitcast_fusion.3, f32[8]{0:T(128)} %fusion.164), channel_id=1, replica_groups=mesh['ep'=8,'seq'=32] {'seq'}, use_global_device_ids=true, to_apply=%region_4.5 | all-reduce | flops 4104 | bytes 32832 | tf_op jit(solution)/shard_map/psum | solution.py:52
  210.4 1.5 fusion.161
  219.9 1.4 fusion.191
  222.1 2.1 fusion.159
  224.3 2.0 fusion.94
  227.7 2.1 fusion.67
  232.4 4.2 collective-permute-start.3
  236.5 1.4 convolution_convert_fusion.1
  238.4 25.7 %fusion.96 = (bf16[704,512]{1,0:T(8,128)(2,1)S(1)}, f32[1,704,512]{2,1,0:T(8,128)S(1)}) fusion(f32[1,704,1024]{2,1,0:T(8,128)} %copy-done.3, f32[704]{0:T(1024)S(1)} %copy-done.15, bf16[1,704,512]{2,1,0:T(8,128)(2,1)} %copy-done.1, bf16[1,15,512]{2,1,0:T(8,128)(2,1)S(1)} %collective-permute-done.3, f32[512]{0:T(512)S(1)} %bitcast.173, f32[512]{0:T(512)S(1)} %bitcast.175, ...), kind=kLoop, calls=%fused_computation.235 | loop fusion | flops 67764224 | bytes 4422400 | tf_op jit(solution)/shard_map/concatenate | solution.py:89
  265.2 2.1 convolution_convert_fusion
  268.5 2.5 fusion.82
  271.1 1.7 fusion.84
  272.8 1.5 fusion.83
  274.3 216.4 %reduce-scatter.11.cloned.1.call-done = bf16[16,512]{1,0:T(8,128)(2,1)} async-done(((bf16[512,512]{1,0:T(8,128)(2,1)}), bf16[16,512]{1,0:T(8,128)(2,1)}) %reduce-scatter.11.cloned.1.call-update) | async-done | bytes 16400 | tf_op jit(solution)/shard_map/reduce_scatter | solution.py:97
  490.6 1.5 copy.28
  492.2 2.2 fusion.68
  494.4 213.8 %reduce-scatter.9.cloned.1.call-done = bf16[16,1024]{1,0:T(8,128)(2,1)} async-done(((bf16[512,1024]{1,0:T(8,128)(2,1)}), bf16[16,1024]{1,0:T(8,128)(2,1)}) %reduce-scatter.9.cloned.1.call-update) | async-done | bytes 32784 | tf_op jit(solution)/shard_map/reduce_scatter | solution.py:94
  708.2 1.6 copy.26
  709.9 1.4 convolution_multiply_fusion.2
  711.3 2.5 stack.127
  715.1 18.4 %psum.44 = bf16[]{:T(256)} all-reduce(bf16[]{:T(256)S(6)} %div.117), channel_id=1, replica_groups=mesh['ep'=8,'seq'=32] {'ep'}, use_global_device_ids=true, to_apply=%region_9.10 | all-reduce | flops 1 | bytes 4 | tf_op jit(solution)/shard_map/psum | solution.py:112
  734.2 44.1 %all-reduce.5.cloned.1.call-done = bf16[512,512]{0,1:T(8,128)(2,1)} async-done(((bf16[512,512]{0,1:T(8,128)(2,1)}), bf16[512,512]{0,1:T(8,128)(2,1)}) %all-reduce.5.cloned.1.call-update) | async-done | bytes 524304 | tf_op jit(solution)/shard_map/psum | solution.py:111
  778.2 2.2 copy.21
  780.4 32.0 %reduce-scatter.15.cloned.1.call-done = bf16[64,16]{1,0:T(8,128)(2,1)} async-done(((bf16[512,16]{1,0:T(8,128)(2,1)}), bf16[64,16]{1,0:T(8,128)(2,1)}) %reduce-scatter.15.cloned.1.call-update) | async-done | bytes 2064
  813.8 33.0 %reduce-scatter.13.cloned.1.call-done = bf16[128,16]{1,0:T(8,128)(2,1)} async-done(((bf16[1024,16]{1,0:T(8,128)(2,1)}), bf16[128,16]{1,0:T(8,128)(2,1)}) %reduce-scatter.13.cloned.1.call-update) | async-done | bytes 4112
  848.3 247.1 %all-reduce.7.cloned.1.call-done = (f32[31,512]{1,0:T(8,128)}, f32[8,512]{1,0:T(8,128)}) async-done(((f32[31,512]{1,0:T(8,128)}, f32[8,512]{1,0:T(8,128)}), (f32[31,512]{1,0:T(8,128)}, f32[8,512]{1,0:T(8,128)})) %all-reduce.7.cloned.1.call-update) | async-done | bytes 79888 | tf_op jit(solution)/shard_map/psum | solution.py:109
  1095.4 1.5 copy.45
  (239 shorter events, 29.7 us)
Async XLA Ops:
  7.2 483.4 %reduce-scatter.11.cloned.1.call-start = ((), (), s32[]{:S(2)}) async-start(), calls=%async_computation.5 | async-start | bytes 540672 | tf_op jit(solution)/shard_map/reduce_scatter | solution.py:97
  12.4 6.8 copy-start.13
  12.4 7.2 copy-start.11
  14.0 6.7 collective-permute-start
  17.9 4.5 collective-permute-start.1
  19.3 12.7 %copy-start.22 = (f32[1,512]{1,0:T(1,128)}, f32[1,512]{1,0:T(1,128)S(1)}, u32[]{:S(2)}) copy-start(f32[1,512]{1,0:T(1,128)S(1)} %get-tuple-element.89) | copy-start | bytes 6148
  19.3 12.7 %copy-start.24 = (f32[1,512]{1,0:T(1,128)}, f32[1,512]{1,0:T(1,128)S(1)}, u32[]{:S(2)}) copy-start(f32[1,512]{1,0:T(1,128)S(1)} %get-tuple-element.90) | copy-start | bytes 6148
  19.4 12.7 %copy-start.26 = (f32[1,512]{1,0:T(1,128)}, f32[1,512]{1,0:T(1,128)S(1)}, u32[]{:S(2)}) copy-start(f32[1,512]{1,0:T(1,128)S(1)} %get-tuple-element.91) | copy-start | bytes 6148
  20.6 11.5 %copy-start.6 = (bf16[1,704,512]{2,1,0:T(8,128)(2,1)S(1)}, bf16[1,704,512]{2,1,0:T(8,128)(2,1)}, u32[]{:S(2)}) copy-start(bf16[1,704,512]{2,1,0:T(8,128)(2,1)} %param.9) | copy-start | bytes 2162692
  20.6 11.5 %copy-start.90 = (bf16[512,512]{1,0:T(8,128)(2,1)S(1)}, bf16[512,512]{1,0:T(8,128)(2,1)}, u32[]{:S(2)}) copy-start(bf16[512,512]{1,0:T(8,128)(2,1)} %param.13) | copy-start | bytes 1572868
  34.1 181.2 %copy-start.10 = (bf16[256,512]{1,0:T(8,128)(2,1)S(1)}, bf16[256,512]{1,0:T(8,128)(2,1)}, u32[]{:S(2)}) copy-start(bf16[256,512]{1,0:T(8,128)(2,1)} %param.16) | copy-start | bytes 786436
  209.5 11.7 %copy-start.12 = (f32[1,8,512]{2,1,0:T(8,128)S(1)}, f32[1,8,512]{2,1,0:T(8,128)}, u32[]{:S(2)}) copy-start(f32[1,8,512]{2,1,0:T(8,128)} %get-tuple-element.60) | copy-start | bytes 49156
  230.8 7.3 collective-permute-start.2
  232.0 6.0 copy-start.15
  232.1 6.0 copy-start.19
  232.1 6.0 copy-start.21
  232.1 6.0 copy-start.23
  232.1 6.0 copy-start.25
  232.1 6.0 copy-start.27
  232.1 6.0 copy-start.29
  232.1 6.0 copy-start.31
  232.1 6.0 copy-start.33
  232.1 6.0 copy-start.35
  232.4 5.7 collective-permute-start.3
  238.0 470.2 %reduce-scatter.9.cloned.1.call-start = ((), (), s32[]{:S(2)}) async-start(), calls=%async_computation.4 | async-start | bytes 1081344 | tf_op jit(solution)/shard_map/reduce_scatter | solution.py:94
  238.1 26.0 %copy-start.4 = (f32[1,704,1024]{2,1,0:T(8,128)S(1)}, f32[1,704,1024]{2,1,0:T(8,128)}, u32[]{:S(2)}) copy-start(f32[1,704,1024]{2,1,0:T(8,128)} %copy-done.3) | copy-start | bytes 8650756
  267.4 510.9 %all-reduce.5.cloned.1.call-start = ((), (), s32[]{:S(2)}) async-start(), calls=%async_computation.6 | async-start | bytes 1048576 | tf_op jit(solution)/shard_map/psum | solution.py:111
  268.5 544.0 %reduce-scatter.15.cloned.1.call-start = ((), (), s32[]{:S(2)}) async-start(), calls=%async_computation.8 | async-start | bytes 147456
  492.1 354.7 %reduce-scatter.13.cloned.1.call-start = ((), (), s32[]{:S(2)}) async-start(), calls=%async_computation.7 | async-start | bytes 294912
  494.4 219.4 %copy-start.84 = (f32[256]{0:T(256)S(1)}, f32[256]{0:T(256)}, u32[]{:S(2)}) copy-start(f32[256]{0:T(256)} %copy-done.83) | copy-start | bytes 3076
  494.4 219.4 %copy-start.87 = (f32[1,256]{1,0:T(1,128)S(1)}, f32[1,256]{1,0:T(1,128)}, u32[]{:S(2)}) copy-start(f32[1,256]{1,0:T(1,128)} %param.17) | copy-start | bytes 3076
  709.8 385.6 %all-reduce.7.cloned.1.call-start = ((), (), s32[]{:S(2)}) async-start(), calls=%async_computation.9 | async-start | bytes 163840 | tf_op jit(solution)/shard_map/psum | solution.py:109
  (70 other events, 251.9 us)
Sparse Core Ops, SparseCore 0:
  238.1 252.4 reduce-scatter.10
  495.5 212.6 reduce-scatter.8
  710.6 67.5 all-reduce.4
  780.6 31.8 reduce-scatter.14
  814.9 31.8 reduce-scatter.12
  852.8 242.5 all-reduce.6
where the time goes:
time: 1110 us
  waiting for transfers between devices  788 us (71%)
  blocking collectives  192 us (17%)
  other arithmetic  55.3 us (5%)
  between operations  20.1 us (2%)
  matrix products  20 us (2%)
  local copies, waits for them, and re-layouts  19.4 us (2%)
    psum x1, waiting for transfers between devices, shards(): grad_kernel, grad_query = lax.psum((kernel_here, query_here), ('ep', 'seq'))  247 us
    reduce_scatter x1, waiting for transfers between devices, shards(): lax.psum_scatter(out_here.astype(jnp.bfloat16), 'seq', scatter_dimension=...  216 us
    reduce_scatter x1, waiting for transfers between devices, shards(): lax.psum_scatter(in_here.astype(jnp.bfloat16), 'seq', scatter_dimension=0...  214 us
    psum x1, blocking collectives, shards(): total, vec = lax.psum((jnp.sum(expo, axis=1), vec_here), 'seq')  111 us
    unnamed x8, waiting for transfers between devices  65.1 us
    pmax x1, blocking collectives, shards(): top = lax.pmax(jnp.max(masked, axis=1), 'seq')  62.9 us
    psum x1, waiting for transfers between devices, shards(): lax.psum(value_here.astype(jnp.bfloat16), 'ep').astype(jnp.float32)  44.1 us
    concatenate x2, other arithmetic, shards(): jnp.concatenate([dglu * sig, dglu * mixed[..., :width] * sig * (1.0 - sig...  26.3 us
  transfers between devices with their start and end apart: 10, of which 7 were waited for; matrix products, arithmetic and copies ran while one was open for 5% of the time, Pallas kernels for 0%

commit v1 on v0

--- a/solution.py
+++ b/solution.py
@@ -106,7 +106,7 @@
             rows_out.astype(jnp.bfloat16), "ep", scatter_dimension=1, tiled=True
         ).astype(jnp.float32),
     )
-    grad_kernel, grad_query = lax.psum((kernel_here, query_here), ("ep", "seq"))
+    grad_kernel, grad_query = lax.psum(lax.psum((kernel_here, query_here), "ep"), "seq")
     grad_value, loss = (
         lax.psum(value_here.astype(jnp.bfloat16), "ep").astype(jnp.float32),
         lax.psum(loss_here.astype(jnp.bfloat16), "ep").astype(jnp.float32),

time: 1110 us -> 871 us (0.78)
  waiting for transfers between devices: 788 us -> 548 us
    psum x1 -> x2, waiting for transfers between devices: 247 us -> 72.7 us  [the longest x1 72.6 us: shards(): lax.psum(lax.psum((kernel_here, query_here), 'ep'), 'seq')]
    psum x1, waiting for transfers between devices: 44.1 us -> 0.03 us  [shards(): lax.psum(value_here.astype(jnp.bfloat16), 'ep').astype(jnp.float32)]
    unnamed x8 -> x9, waiting for transfers between devices: 65.1 us -> 45.9 us
  transfers between devices with their start and end apart: 10 -> 11, of which waited for: 7 -> 6; matrix products, arithmetic and copies ran while one was open for 5% -> 6% of each run, Pallas kernels for 0% -> 0%
where the time goes in v1:
time: 871 us; the launch traced here: 866 us
  waiting for transfers between devices  548 us (63%)
  blocking collectives  192 us (22%)
  other arithmetic  54.3 us (6%)
  between operations  21.5 us (2%)
  matrix products  20 us (2%)
  local copies, waits for them, and re-layouts  19.4 us (2%)
  starting transfers between devices  11 us (1%)
    reduce_scatter x1, waiting for transfers between devices, shards(): lax.psum_scatter(in_here.astype(jnp.bfloat16), 'seq', scatter_dimension=0...  216 us
    reduce_scatter x1, waiting for transfers between devices, shards(): lax.psum_scatter(out_here.astype(jnp.bfloat16), 'seq', scatter_dimension=...  211 us
    psum x1, blocking collectives, shards(): total, vec = lax.psum((jnp.sum(expo, axis=1), vec_here), 'seq')  111 us
    psum x1, waiting for transfers between devices, shards(): lax.psum(lax.psum((kernel_here, query_here), 'ep'), 'seq')  72.6 us
    pmax x1, blocking collectives, shards(): top = lax.pmax(jnp.max(masked, axis=1), 'seq')  62.9 us
    unnamed x9, waiting for transfers between devices  45.9 us
    concatenate x2, other arithmetic, shards(): jnp.concatenate([dglu * sig, dglu * mixed[..., :width] * sig * (1.0 - sig...  26.3 us
    psum x1, blocking collectives, shards(): lax.psum(loss_here.astype(jnp.bfloat16), 'ep').astype(jnp.float32)  18.1 us
  transfers between devices with their start and end apart: 11, of which 6 were waited for; matrix products, arithmetic and copies ran while one was open for 6% of the time, Pallas kernels for 0%

profile of v1, /device:TPU:1, one launch (start us, length us, event | category | flops | bytes accessed | tf_op | source)
XLA Modules:
  0.0 866.0 jit_solution(17126749846028417517)
XLA Ops:
  10.2 1.5 fusion.5
  14.8 3.9 collective-permute-start
  21.5 1.8 collective-permute-done.1
  23.5 9.4 %fusion.36 = f32[1,704,512]{2,1,0:T(8,128)S(1)} fusion(bf16[1,704,512]{2,1,0:T(8,128)(2,1)S(1)} %multiply_convert_fusion.3, bf16[1,15,512]{2,1,0:T(8,128)(2,1)S(1)} %collective-permute-done.1, bf16[1,15,512]{2,1,0:T(8,128)(2,1)S(1)} %collective-permute-done, f32[512]{0:T(512)S(1)} %bitcast.172, f32[512]{0:T(512)S(1)} %bitcast.174, f32[512]{0:T(512)S(1)} %bitcast.178, ...), kind=kLoop, calls=%fused_computation.163 | loop fusion | flops 65601536 | bytes 2256896 | tf_op jit(solution)/shard_map/add | solution.py:42
  34.9 62.9 %pmax.7 = f32[8]{0:T(128)S(1)} all-reduce(f32[8]{0:T(128)S(1)} %get-tuple-element.103), channel_id=1, replica_groups=mesh['ep'=8,'seq'=32] {'seq'}, use_global_device_ids=true, to_apply=%region_3.4 | all-reduce | flops 8 | bytes 64 | tf_op jit(solution)/shard_map/pmax | solution.py:49
  99.3 111.0 %all-reduce.1 = (f32[1,8,512]{2,1,0:T(8,128)}, f32[8]{0:T(128)S(1)}) all-reduce(f32[1,8,512]{2,1,0:T(8,128)S(1)} %convolution_bitcast_fusion.3, f32[8]{0:T(128)} %fusion.164), channel_id=1, replica_groups=mesh['ep'=8,'seq'=32] {'seq'}, use_global_device_ids=true, to_apply=%region_4.5 | all-reduce | flops 4104 | bytes 32832 | tf_op jit(solution)/shard_map/psum | solution.py:52
  211.2 1.5 fusion.161
  220.7 1.4 fusion.191
  223.0 2.1 fusion.159
  225.1 2.0 fusion.94
  228.6 2.2 fusion.67
  233.2 4.2 collective-permute-start.3
  237.4 1.4 convolution_convert_fusion.1
  239.3 25.7 %fusion.96 = (bf16[704,512]{1,0:T(8,128)(2,1)S(1)}, f32[1,704,512]{2,1,0:T(8,128)S(1)}) fusion(f32[1,704,1024]{2,1,0:T(8,128)} %copy-done.3, f32[704]{0:T(1024)S(1)} %copy-done.15, bf16[1,704,512]{2,1,0:T(8,128)(2,1)} %copy-done.1, bf16[1,15,512]{2,1,0:T(8,128)(2,1)S(1)} %collective-permute-done.3, f32[512]{0:T(512)S(1)} %bitcast.173, f32[512]{0:T(512)S(1)} %bitcast.175, ...), kind=kLoop, calls=%fused_computation.235 | loop fusion | flops 67764224 | bytes 4422400 | tf_op jit(solution)/shard_map/concatenate | solution.py:89
  266.1 2.1 convolution_convert_fusion
  268.4 2.3 fusion.68
  270.7 1.5 fusion.82
  272.1 1.5 fusion.83
  273.6 1.7 fusion.84
  275.3 2.5 stack.127
  277.9 1.4 convolution_multiply_fusion.2
  280.4 211.1 %reduce-scatter.11.cloned.1.call-done = bf16[16,512]{1,0:T(8,128)(2,1)} async-done(((bf16[512,512]{1,0:T(8,128)(2,1)}), bf16[16,512]{1,0:T(8,128)(2,1)}) %reduce-scatter.11.cloned.1.call-update) | async-done | bytes 16400 | tf_op jit(solution)/shard_map/reduce_scatter | solution.py:97
  491.5 1.5 copy.28
  493.0 216.3 %reduce-scatter.9.cloned.1.call-done = bf16[16,1024]{1,0:T(8,128)(2,1)} async-done(((bf16[512,1024]{1,0:T(8,128)(2,1)}), bf16[16,1024]{1,0:T(8,128)(2,1)}) %reduce-scatter.9.cloned.1.call-update) | async-done | bytes 32784 | tf_op jit(solution)/shard_map/reduce_scatter | solution.py:94
  709.3 1.6 copy.26
  712.8 18.1 %psum.58 = bf16[]{:T(256)} all-reduce(bf16[]{:T(256)S(6)} %div.117), channel_id=1, replica_groups=mesh['ep'=8,'seq'=32] {'ep'}, use_global_device_ids=true, to_apply=%region_9.10 | all-reduce | flops 1 | bytes 4 | tf_op jit(solution)/shard_map/psum | solution.py:112
  731.6 2.2 copy.21
  733.9 12.5 %reduce-scatter.15.cloned.1.call-done = bf16[64,16]{1,0:T(8,128)(2,1)} async-done(((bf16[512,16]{1,0:T(8,128)(2,1)}), bf16[64,16]{1,0:T(8,128)(2,1)}) %reduce-scatter.15.cloned.1.call-update) | async-done | bytes 2064
  747.7 32.9 %reduce-scatter.13.cloned.1.call-done = bf16[128,16]{1,0:T(8,128)(2,1)} async-done(((bf16[1024,16]{1,0:T(8,128)(2,1)}), bf16[128,16]{1,0:T(8,128)(2,1)}) %reduce-scatter.13.cloned.1.call-update) | async-done | bytes 4112
  782.1 72.6 %all-reduce.9.cloned.1.call-done = (f32[31,512]{1,0:T(8,128)}, f32[8,512]{1,0:T(8,128)}) async-done(((f32[31,512]{1,0:T(8,128)}, f32[8,512]{1,0:T(8,128)}), (f32[31,512]{1,0:T(8,128)}, f32[8,512]{1,0:T(8,128)})) %all-reduce.9.cloned.1.call-update) | async-done | bytes 79888 | tf_op jit(solution)/shard_map/psum | solution.py:109
  854.7 1.5 copy.47
  856.2 1.3 copy.48
  (242 shorter events, 29.0 us)
Async XLA Ops:
  8.0 483.5 %reduce-scatter.11.cloned.1.call-start = ((), (), s32[]{:S(2)}) async-start(), calls=%async_computation.5 | async-start | bytes 540672 | tf_op jit(solution)/shard_map/reduce_scatter | solution.py:97
  13.2 6.8 copy-start.13
  13.2 7.2 copy-start.11
  14.8 6.7 collective-permute-start
  18.7 4.5 collective-permute-start.1
  20.2 12.7 %copy-start.22 = (f32[1,512]{1,0:T(1,128)}, f32[1,512]{1,0:T(1,128)S(1)}, u32[]{:S(2)}) copy-start(f32[1,512]{1,0:T(1,128)S(1)} %get-tuple-element.91) | copy-start | bytes 6148
  20.2 12.7 %copy-start.24 = (f32[1,512]{1,0:T(1,128)}, f32[1,512]{1,0:T(1,128)S(1)}, u32[]{:S(2)}) copy-start(f32[1,512]{1,0:T(1,128)S(1)} %get-tuple-element.92) | copy-start | bytes 6148
  20.2 12.7 %copy-start.26 = (f32[1,512]{1,0:T(1,128)}, f32[1,512]{1,0:T(1,128)S(1)}, u32[]{:S(2)}) copy-start(f32[1,512]{1,0:T(1,128)S(1)} %get-tuple-element.93) | copy-start | bytes 6148
  21.5 11.5 %copy-start.6 = (bf16[1,704,512]{2,1,0:T(8,128)(2,1)S(1)}, bf16[1,704,512]{2,1,0:T(8,128)(2,1)}, u32[]{:S(2)}) copy-start(bf16[1,704,512]{2,1,0:T(8,128)(2,1)} %param.9) | copy-start | bytes 2162692
  21.5 11.5 %copy-start.90 = (bf16[512,512]{1,0:T(8,128)(2,1)S(1)}, bf16[512,512]{1,0:T(8,128)(2,1)}, u32[]{:S(2)}) copy-start(bf16[512,512]{1,0:T(8,128)(2,1)} %param.13) | copy-start | bytes 1572868
  34.9 181.2 %copy-start.10 = (bf16[256,512]{1,0:T(8,128)(2,1)S(1)}, bf16[256,512]{1,0:T(8,128)(2,1)}, u32[]{:S(2)}) copy-start(bf16[256,512]{1,0:T(8,128)(2,1)} %param.16) | copy-start | bytes 786436
  210.3 11.7 %copy-start.12 = (f32[1,8,512]{2,1,0:T(8,128)S(1)}, f32[1,8,512]{2,1,0:T(8,128)}, u32[]{:S(2)}) copy-start(f32[1,8,512]{2,1,0:T(8,128)} %get-tuple-element.60) | copy-start | bytes 49156
  231.6 7.4 collective-permute-start.2
  232.9 6.1 copy-start.15
  232.9 6.1 copy-start.19
  232.9 6.1 copy-start.21
  232.9 6.1 copy-start.23
  232.9 6.1 copy-start.25
  232.9 6.1 copy-start.27
  232.9 6.1 copy-start.29
  233.0 6.1 copy-start.31
  233.0 6.1 copy-start.33
  233.2 5.8 collective-permute-start.3
  238.9 470.4 %reduce-scatter.9.cloned.1.call-start = ((), (), s32[]{:S(2)}) async-start(), calls=%async_computation.4 | async-start | bytes 1081344 | tf_op jit(solution)/shard_map/reduce_scatter | solution.py:94
  239.0 26.0 %copy-start.4 = (f32[1,704,1024]{2,1,0:T(8,128)S(1)}, f32[1,704,1024]{2,1,0:T(8,128)}, u32[]{:S(2)}) copy-start(f32[1,704,1024]{2,1,0:T(8,128)} %copy-done.3) | copy-start | bytes 8650756
  268.3 442.7 %all-reduce.11.cloned.1.call-start = ((), (), s32[]{:S(2)}) async-start(), calls=%async_computation.10 | async-start | bytes 163840 | tf_op jit(solution)/shard_map/psum | solution.py:109
  277.9 433.6 %copy-start.84 = (f32[256]{0:T(256)S(1)}, f32[256]{0:T(256)}, u32[]{:S(2)}) copy-start(f32[256]{0:T(256)} %copy-done.83) | copy-start | bytes 3076
  277.9 433.7 %copy-start.87 = (f32[1,256]{1,0:T(1,128)S(1)}, f32[1,256]{1,0:T(1,128)}, u32[]{:S(2)}) copy-start(f32[1,256]{1,0:T(1,128)} %param.17) | copy-start | bytes 3076
  279.3 452.3 %all-reduce.7.cloned.1.call-start = ((), (), s32[]{:S(2)}) async-start(), calls=%async_computation.6 | async-start | bytes 1048576 | tf_op jit(solution)/shard_map/psum | solution.py:111
  280.3 466.0 %reduce-scatter.15.cloned.1.call-start = ((), (), s32[]{:S(2)}) async-start(), calls=%async_computation.8 | async-start | bytes 147456
  493.0 287.6 %reduce-scatter.13.cloned.1.call-start = ((), (), s32[]{:S(2)}) async-start(), calls=%async_computation.7 | async-start | bytes 294912
  710.9 143.8 %all-reduce.9.cloned.1.call-start = ((), (), s32[]{:S(2)}) async-start(), calls=%async_computation.9 | async-start | bytes 163840 | tf_op jit(solution)/shard_map/psum | solution.py:109
  (71 other events, 259.6 us)
Sparse Core Ops, SparseCore 0:
  239.0 252.4 reduce-scatter.10
  496.4 212.8 reduce-scatter.8
  712.0 34.3 reduce-scatter.14
  748.7 31.9 reduce-scatter.12
Sparse Core Ops, SparseCore 1:
  279.4 108.4 all-reduce.10
  390.1 63.9 all-reduce.6
  715.3 139.3 all-reduce.8
